TPU v7x, 1024 devices: a whole 4x4x32 slice. The times are simulated.
1024 devices in a mesh: node: 32 (over z_hi, x, core), local: 32 (over z_lo, y).
Axes of the slice: x: 4, y: 4, z: 32 (z_hi: 4, z_lo: 8; z = z_hi * 8 + z_lo), core: 2. Of those that a mesh axis runs over, the one named last changes fastest.
Arguments:
- d_out: bfloat16 [4096, 7168], P('node', 'local'), may hold values from -6 to 6
- combine: float32 [4096, 3], P('node'), may hold values from 0.05 to 1
- expert_ids: int32 [4096, 3], P('node'), may hold values from 0 to 31, as said below
- slot_ids: int32 [4096, 3], P('node'), may hold values from -1 to 11, as said below
- w_gate: bfloat16 [32, 7168, 2048], P('node', 'local'), may hold values from -0.0625 to 0.0625
- w_up: bfloat16 [32, 7168, 2048], P('node', 'local'), may hold values from -0.0625 to 0.0625
- w_down: bfloat16 [32, 2048, 7168], P('node', None, 'local'), may hold values from -0.125 to 0.125
- saved_gate: bfloat16 [32, 384, 2048], P('node'), may hold values from -6 to 6
- saved_up: bfloat16 [32, 384, 2048], P('node'), may hold values from -6 to 6
Outputs:
- d_input: bfloat16 [4096, 7168], P('node', 'local')
Inputs may be any that keep to these rules, and one draw needn't show every extreme that they name: `expert_ids`: each token names 3 different experts. `slot_ids`: picks of one source node at one expert hold distinct slots, numbered in the order of the tokens; -1 marks a pick beyond the 12 rows of that block, which is dropped; in every draw some source node fills all 12 rows at some expert.
All inputs are finite; a program needn't handle non-finite values.
Results may differ from a plain program's by a relative error of at most 0.034.
Values may be sent and summed in bfloat16 or wider, within the bound.
A program may use at most 32 MiB of HBM per device.

v0:
```python
import jax
import jax.numpy as jnp
from jax import lax
from jax.sharding import PartitionSpec as P


def swiglu_back(grad_hidden, gate_value, up_value):
    gate_float = gate_value.astype(jnp.float32)
    up_float = up_value.astype(jnp.float32)
    sigmoid_gate = jax.nn.sigmoid(gate_float)
    grad_gate = grad_hidden * up_float * sigmoid_gate * (1.0 + gate_float * (1.0 - sigmoid_gate))
    grad_up = grad_hidden * gate_float * sigmoid_gate
    return (grad_gate.astype(jnp.bfloat16), grad_up.astype(jnp.bfloat16))


def on_device(d_out, combine, expert_ids, slot_ids, w_gate, w_up, w_down, saved_gate, saved_up):
    node_count = lax.axis_size("node")
    tok_rows = d_out.shape[0]
    feat_width = d_out.shape[1]
    slot_total = saved_gate.shape[1]
    capacity = slot_total // node_count
    is_kept = slot_ids >= 0
    slot_place = jnp.where(is_kept, expert_ids * capacity + slot_ids, slot_total)
    token_index = jnp.broadcast_to(jnp.arange(tok_rows, dtype=jnp.int32)[:, None], slot_place.shape)
    slot_owner = (
        jnp.zeros((slot_total + 1,), jnp.int32)
        .at[slot_place.reshape(-1)]
        .set(token_index.reshape(-1))[:slot_total]
    )
    slot_weight = (
        jnp.zeros((slot_total + 1,), jnp.float32)
        .at[slot_place.reshape(-1)]
        .set(combine.reshape(-1))[:slot_total]
    )
    outgoing = (d_out[slot_owner].astype(jnp.float32) * slot_weight[:, None]).astype(jnp.bfloat16)
    outgoing = outgoing.reshape(node_count, capacity, feat_width)
    arrived = lax.all_to_all(outgoing, "node", split_axis=0, concat_axis=0, tiled=True).reshape(
        slot_total, feat_width
    )
    partial_value = lax.dot_general(
        arrived, w_down[0], (((1,), (1,)), ((), ())), preferred_element_type=jnp.float32
    )
    hidden_share = lax.psum_scatter(
        partial_value.astype(jnp.bfloat16), "local", scatter_dimension=1, tiled=True
    ).astype(jnp.float32)
    share_width = hidden_share.shape[1]
    col_start = lax.axis_index("local") * share_width
    gate_share = lax.dynamic_slice_in_dim(saved_gate[0], col_start, share_width, 1)
    up_share = lax.dynamic_slice_in_dim(saved_up[0], col_start, share_width, 1)
    grad_gate, grad_up = swiglu_back(hidden_share, gate_share, up_share)
    grad_gate, grad_up = (
        lax.all_gather(grad_gate, "local", axis=1, tiled=True),
        lax.all_gather(grad_up, "local", axis=1, tiled=True),
    )
    grad_rows = lax.dot_general(
        grad_gate, w_gate[0], (((1,), (1,)), ((), ())), preferred_element_type=jnp.float32
    )
    grad_rows = grad_rows + lax.dot_general(
        grad_up, w_up[0], (((1,), (1,)), ((), ())), preferred_element_type=jnp.float32
    )
    grad_rows = grad_rows.astype(jnp.bfloat16).reshape(node_count, capacity, feat_width)
    returned = lax.all_to_all(grad_rows, "node", split_axis=0, concat_axis=0, tiled=True)
    returned_flat = returned.reshape(slot_total, feat_width)
    pick_index = jnp.where(is_kept, slot_place, 0)
    picked = returned_flat[pick_index].astype(jnp.float32) * is_kept[..., None].astype(jnp.float32)
    return jnp.sum(picked, axis=1).astype(jnp.bfloat16)


def solution(mesh):
    return jax.shard_map(
        on_device,
        mesh=mesh,
        in_specs=(
            P("node", "local"),
            P("node", None),
            P("node", None),
            P("node", None),
            P("node", "local", None),
            P("node", "local", None),
            P("node", None, "local"),
            P("node", None, None),
            P("node", None, None),
        ),
        out_specs=P("node", "local"),
        check_vma=False,
    )
```

profile of v0, /device:TPU:1, one launch (start us, length us, event | category | flops | bytes accessed | tf_op | source)
XLA Modules:
  0.0 858.4 jit_solution(2757747143977504492)
XLA Ops:
  6.5 0.8 compare_select_fusion.1
  7.3 0.1 copy.32
  7.5 0.2 reshape.65
  7.7 0.2 reshape.94
  7.9 2.9 scatter_custom_fusion
  10.8 0.9 copy.33
  11.8 2.1 gather_fusion
  13.9 0.1 copy.34
  14.0 0.2 reshape.102
  14.2 2.9 scatter_custom_fusion.1
  17.2 0.1 multiply_convert_fusion
  17.4 67.3 %all_to_all.10 = bf16[32,12,224]{2,1,0:T(8,128)(2,1)S(1)} all-to-all(bf16[32,12,224]{2,1,0:T(8,128)(2,1)S(1)} %multiply_convert_fusion), channel_id=1, replica_groups=mesh['node'=32,'local'=32] {'node'}, dimensions={0} | all-to-all | bytes 344064 | tf_op jit(solution)/shard_map/all_to_all | solution.py:37
  84.8 1.9 convolution_convert_fusion
  86.8 1.1 constant_dynamic-slice_fusion
  88.1 217.7 %reduce-scatter.2.cloned.1.call-done = bf16[384,64]{0,1:T(8,128)(2,1)} async-done(((bf16[384,2048]{0,1:T(8,128)(2,1)}), bf16[384,64]{0,1:T(8,128)(2,1)}) %reduce-scatter.2.cloned.1.call-update) | async-done | bytes 49168 | tf_op jit(solution)/shard_map/reduce_scatter | solution.py:43
  305.8 1.5 fusion.13
  307.3 0.7 all-gather.5.cloned.1.call-update
  308.0 229.3 %all-gather.3.cloned.1.call-done = bf16[384,2048]{0,1:T(8,128)(2,1)} async-done(((bf16[384,64]{0,1:T(8,128)(2,1)}), bf16[384,2048]{0,1:T(8,128)(2,1)}) %all-gather.3.cloned.1.call-update) | async-done | bytes 1572880 | tf_op jit(solution)/shard_map/all_gather | solution.py:52
  537.3 2.1 fusion.2
  539.4 232.5 %all-gather.5.cloned.1.call-done = bf16[384,2048]{0,1:T(8,128)(2,1)} async-done(((bf16[384,64]{0,1:T(8,128)(2,1)}), bf16[384,2048]{0,1:T(8,128)(2,1)}) %all-gather.5.cloned.1.call-update) | async-done | bytes 1572880 | tf_op jit(solution)/shard_map/all_gather | solution.py:53
  772.0 2.1 fusion
  774.0 0.1 copy.37
  774.2 0.8 reshape.69
  774.9 46.6 %all-to-all-start.1 = ((bf16[32,12,224]{2,1,0:T(8,128)(2,1)}), bf16[32,12,224]{2,1,0:T(8,128)(2,1)S(1)}, u32[]{:S(2)}, u32[]{:S(2)}) async-start(bf16[32,12,224]{2,1,0:T(8,128)(2,1)} %reshape.69), calls=%async_computation.2 | async-start | bytes 524288 | tf_op jit(solution)/shard_map/all_to_all | solution.py:62
  821.5 0.1 copy.38
  821.6 0.2 reshape.84
  821.9 0.1 copy.39
  822.0 26.4 %all-to-all-done.1 = bf16[32,12,224]{2,1,0:T(8,128)(2,1)S(1)} async-done(((bf16[32,12,224]{2,1,0:T(8,128)(2,1)}), bf16[32,12,224]{2,1,0:T(8,128)(2,1)S(1)}, u32[]{:S(2)}, u32[]{:S(2)}) %all-to-all-start.1) | async-done | bytes 172064 | tf_op jit(solution)/shard_map/all_to_all | solution.py:62
  848.5 2.1 gather_fusion.1
  850.5 0.2 reshape.109
  850.7 0.4 multiply_reduce_fusion
  851.2 0.7 copy.40
  (27 shorter events, 0.7 us)
Async XLA Ops:
  6.5 78.2 %copy-start = (bf16[1,2048,224]{1,2,0:T(8,128)(2,1)S(1)}, bf16[1,2048,224]{1,2,0:T(8,128)(2,1)}, u32[]{:S(2)}) copy-start(bf16[1,2048,224]{1,2,0:T(8,128)(2,1)} %param.15) | copy-start | bytes 2752516
  6.5 7.3 copy-start.4
  6.5 299.2 %reduce-scatter.2.cloned.1.call-start = ((), (), s32[]{:S(2)}) async-start(), calls=%async_computation.3 | async-start | bytes 1622016 | tf_op jit(solution)/shard_map/reduce_scatter | solution.py:43
  86.7 450.7 %copy-start.1 = (bf16[1,224,2048]{2,1,0:T(8,128)(2,1)S(1)}, bf16[1,224,2048]{2,1,0:T(8,128)(2,1)}, u32[]{:S(2)}) copy-start(bf16[1,224,2048]{2,1,0:T(8,128)(2,1)} %param.13) | copy-start | bytes 2752516
  86.7 450.6 %all-gather.3.cloned.1.call-start = ((), (), s32[]{:S(2)}) async-start(), calls=%async_computation.4 | async-start | bytes 1622016 | tf_op jit(solution)/shard_map/all_gather | solution.py:52
  88.1 683.8 %copy-start.2 = (bf16[1,224,2048]{2,1,0:T(8,128)(2,1)S(1)}, bf16[1,224,2048]{2,1,0:T(8,128)(2,1)}, u32[]{:S(2)}) copy-start(bf16[1,224,2048]{2,1,0:T(8,128)(2,1)} %param.14) | copy-start | bytes 2752516
  307.3 464.7 %all-gather.5.cloned.1.call-start = ((), (), s32[]{:S(2)}) async-start(), calls=%async_computation.5 | async-start | bytes 1622016 | tf_op jit(solution)/shard_map/all_gather | solution.py:53
  539.4 282.4 %copy-start.3 = (s32[128,3]{0,1:T(4,128)S(1)}, s32[128,3]{0,1:T(4,128)}, u32[]{:S(2)}) copy-start(s32[128,3]{0,1:T(4,128)} %param.12) | copy-start | bytes 4612
  774.9 73.4 %all-to-all-start.1 = ((bf16[32,12,224]{2,1,0:T(8,128)(2,1)}), bf16[32,12,224]{2,1,0:T(8,128)(2,1)S(1)}, u32[]{:S(2)}, u32[]{:S(2)}) async-start(bf16[32,12,224]{2,1,0:T(8,128)(2,1)} %reshape.69), calls=%async_computation.2 | async-start | bytes 524288 | tf_op jit(solution)/shard_map/all_to_all | solution.py:62
Sparse Core Ops, SparseCore 0:
  86.8 218.9 reduce-scatter.1
  308.8 228.4 all-gather.2
  540.3 231.5 all-gather.4
where the time goes:
time: 859 us; the launch traced here: 858 us
  waiting for transfers between devices  707 us (82%)
  blocking collectives  67.3 us (8%)
  starting transfers between devices  46.7 us (5%)
  local copies, waits for them, and re-layouts  15.6 us (2%)
  between operations  13.3 us (2%)
    all_gather x1, waiting for transfers between devices, on_device(): lax.all_gather(grad_up, 'local', axis=1, tiled=True)  233 us
    all_gather x1, waiting for transfers between devices, on_device(): lax.all_gather(grad_gate, 'local', axis=1, tiled=True)  229 us
    reduce_scatter x1, waiting for transfers between devices, on_device(): lax.psum_scatter(partial_value.astype(jnp.bfloat16), 'local', scatter_dim...  218 us
    all_to_all x1, blocking collectives, on_device(): lax.all_to_all(outgoing, 'node', split_axis=0, concat_axis=0, tiled=True)  67.3 us
    all_to_all x1, starting transfers between devices, on_device(): lax.all_to_all(grad_rows, 'node', split_axis=0, concat_axis=0, tiled=True)  46.6 us
    all_to_all x1, waiting for transfers between devices, on_device(): lax.all_to_all(grad_rows, 'node', split_axis=0, concat_axis=0, tiled=True)  26.4 us
  transfers between devices with their start and end apart: 4, of which 4 were waited for; matrix products, arithmetic and copies ran while one was open for 0% of the time, Pallas kernels for 0%

commit v1 on v0

v1 whole, which is shorter than its diff:
```python
import functools

import jax
import jax.numpy as jnp
import numpy as np
from jax import lax
from jax.experimental import pallas as pl
from jax.experimental.pallas import tpu as pltpu
from jax.sharding import PartitionSpec as P

F32, BF16 = jnp.float32, jnp.bfloat16
GROUPS, PEERS, CAP = 4, 8, 12
ROWS = PEERS * CAP
PART = GROUPS * CAP
SLOTS = GROUPS * ROWS
ORDER = (0, 1, 3, 2)
LAG = (0, 3, 4, 7)
STAGES = 11
NCOPY = 3 + 7 + 3 + 7 + GROUPS * 14


def mul(value, unit):
    return pl.multiple_of(value, unit)


def contract(a, b):
    return lax.dot_general(a, b, (((1,), (1,)), ((), ())), preferred_element_type=F32)


def kernel(
    d_out, place_row, weight_row, place_col, perm_out, perm_back, wg_hbm, wu_hbm, wd_hbm, sg_hbm, su_hbm,
    result,
    wg, wu, wd, sg, su, fac_g, fac_u, out, x1, zsend, arr, part, r1, ys2, t2, r2, zs1, z1, u1, zs2, z2, u2, zs3, z3, u3,
    dh, gr, ret, snd, rx, pick, load_sem, send_sem, recv_sem,
):
    hid, feat = wd.shape
    node, local = lax.axis_index("node"), lax.axis_index("local")
    zh, j = lax.div(node, PEERS), lax.rem(node, PEERS)
    zl, y = lax.div(local, 4), lax.rem(local, 4)
    ya = y + 1 - 2 * lax.rem(y, 2)
    yb = 3 - y
    b0, b1, b2 = lax.rem(zl, 2), lax.rem(lax.div(zl, 2), 2), lax.div(zl, 4)
    to_z1, to_z2, to_z3 = zl + 1 - 2 * b0, zl + 2 - 4 * b1, zl + 4 - 8 * b2
    half = (lax.rem(lax.div(y + 1, 2), 2), lax.div(y, 2))
    quarter = (lax.div(y, 2), lax.rem(y, 2))
    first_to, second_to = (ya, yb), (yb, ya)
    own1 = [s * (hid // 2) + half[s] * (hid // 4) for s in range(2)]
    other1 = [s * (hid // 2) + (1 - half[s]) * (hid // 4) for s in range(2)]
    own2 = [own1[s] + quarter[s] * (hid // 8) for s in range(2)]
    other2 = [own1[s] + (1 - quarter[s]) * (hid // 8) for s in range(2)]
    own3 = own2[0] + b0 * (own2[1] - own2[0])
    own4 = own3 + b1 * (hid // 16)
    w4, w8, w16 = hid // 4, hid // 8, hid // 16

    def cols(start, size):
        return pl.ds(mul(start, 128), size)

    def peer(k):
        return {"node": zh * PEERS + k, "local": local}

    def group(k):
        return {"node": k * PEERS + j, "local": local}

    def at_y(k):
        return {"node": node, "local": zl * 4 + k}

    def at_z(k):
        return {"node": node, "local": k * 4 + y}

    loads = [
        pltpu.make_async_copy(src, dst, load_sem.at[i])
        for i, (src, dst) in enumerate(((wd_hbm, wd), (sg_hbm, sg), (su_hbm, su), (wg_hbm, wg), (wu_hbm, wu)))
    ]
    for load in loads:
        load.start()

    barrier = pltpu.get_barrier_semaphore()
    partners = [peer(lax.rem(j + o, PEERS)) for o in range(1, PEERS)]
    partners += [group(lax.rem(zh + d, GROUPS)) for d in range(1, GROUPS)]
    partners += [at_y(ya), at_y(yb), at_z(to_z1), at_z(to_z2), at_z(to_z3)]
    for partner in partners:
        pl.semaphore_signal(barrier, inc=1, device_id=partner, device_id_type=pl.DeviceIdType.MESH)

    slot = lax.broadcasted_iota(jnp.int32, (SLOTS, d_out.shape[0]), 0)
    chosen = jnp.zeros(slot.shape, F32)
    weight = jnp.zeros(slot.shape, F32)
    for k in range(3):
        hit = slot == place_row[k : k + 1, :]
        chosen = chosen + jnp.where(hit, 1.0, 0.0)
        weight = weight + jnp.where(hit, weight_row[k : k + 1, :], 0.0)
    weight = jnp.sum(weight, axis=1, keepdims=True)
    rows = jnp.dot(chosen.astype(BF16), d_out[...], preferred_element_type=F32)
    out[...] = (rows * weight).astype(BF16)

    pl.semaphore_wait(barrier, len(partners))

    started = []

    def send(src, dst, to):
        i = len(started)
        copy = pltpu.make_async_remote_copy(
            src_ref=src, dst_ref=dst, send_sem=send_sem.at[i], recv_sem=recv_sem.at[i],
            device_id=to, device_id_type=pl.DeviceIdType.MESH,
        )
        copy.start()
        started.append(copy)
        return copy

    def piece(k):
        return pl.ds(mul(k * PART, 16), PART)

    to_peers = [
        send(out.at[piece(lax.rem(j + o, PEERS))], x1.at[piece(j)], peer(lax.rem(j + o, PEERS)))
        for o in range(1, PEERS)
    ]
    x1[piece(j), :] = out[piece(j), :]
    where = lax.broadcasted_iota(jnp.int32, pick.shape, 1)
    picked = jnp.zeros(pick.shape, F32)
    for k in range(3):
        picked = picked + jnp.where(where == place_col[:, k : k + 1], 1.0, 0.0)
    pick[...] = picked.astype(BF16)
    for copy in to_peers:
        copy.wait_recv()
    sorted_rows = jnp.dot(perm_out[...], x1[...], preferred_element_type=F32).astype(BF16)
    for d in range(GROUPS):
        block = sorted_rows[d * ROWS : (d + 1) * ROWS]
        if d == 0:
            arr[0] = block
        else:
            zsend[d] = block
    to_groups = {}
    for d in ORDER[1:]:
        to_groups[d] = send(zsend.at[d], arr.at[d], group(lax.rem(zh + d, GROUPS)))
    loads[0].wait()

    def factors(d):
        base = lax.rem(zh - d + GROUPS, GROUPS) * ROWS

        def step(i, carry):
            r = pl.ds(mul(base + i * 16, 16), 16)
            gate, up = sg[r, :].astype(F32), su[r, :].astype(F32)
            sig = 1.0 / (1.0 + jnp.exp(-gate))
            to = pl.ds(mul(i * 16, 16), 16)
            fac_g[d, to, :] = up * sig * (1.0 + gate * (1.0 - sig))
            fac_u[d, to, :] = gate * sig
            return carry

        lax.fori_loop(0, ROWS // 16, step, 0)

    pending = {}
    returned = {}

    def stage(d, s):
        if s == 0:
            if d:
                to_groups[d].wait_recv()

            def mat(i, carry):
                c = cols(i * w4, w4)
                part[d, :, c] = contract(arr[d], wd[pl.ds(mul(i * w4, 128), w4), :]).astype(BF16)
                return carry

            lax.fori_loop(0, 4, mat, 0)
            pending[d] = [send(part.at[d, :, cols(other1[k], w4)], r1.at[d, k], at_y(first_to[k])) for k in range(2)]
            if d == 0:
                loads[1].wait()
                loads[2].wait()
            factors(d)
            return
        for copy in pending[d]:
            copy.wait_recv()
        if s == 1:
            pending[d] = []
            for k in range(2):
                ys2[d, k] = (
                    part[d, :, cols(other2[k], w8)].astype(F32)
                    + r1[d, k, :, cols((1 - quarter[k]) * w8, w8)].astype(F32)
                ).astype(BF16)
                pending[d].append(send(ys2.at[d, k], r2.at[d, k], at_y(second_to[k])))
            for k in range(2):
                t2[d, k] = part[d, :, cols(own2[k], w8)].astype(F32) + r1[d, k, :, cols(quarter[k] * w8, w8)].astype(F32)
        elif s == 2:
            zs1[d] = (t2[d, 1 - b0] + r2[d, 1 - b0].astype(F32)).astype(BF16)
            pending[d] = [send(zs1.at[d], z1.at[d], at_z(to_z1))]
            u1[d] = t2[d, b0] + r2[d, b0].astype(F32)
        elif s == 3:
            far, near = cols((1 - b1) * w16, w16), cols(b1 * w16, w16)
            zs2[d] = (u1[d, :, far] + z1[d, :, far].astype(F32)).astype(BF16)
            pending[d] = [send(zs2.at[d], z2.at[d], at_z(to_z2))]
            u2[d] = u1[d, :, near] + z1[d, :, near].astype(F32)
        elif s == 4:
            far, near = pl.ds(mul((1 - b2) * 48, 16), 48), pl.ds(mul(b2 * 48, 16), 48)
            zs3[d] = (u2[d, far, :] + z2[d, far, :].astype(F32)).astype(BF16)
            pending[d] = [send(zs3.at[d], z3.at[d], at_z(to_z3))]
            u3[d] = u2[d, near, :] + z2[d, near, :].astype(F32)
        elif s == 5:
            r, c = pl.ds(mul(b2 * 48, 16), 48), cols(own4, w16)
            dh[d, r, c] = (u3[d] + z3[d].astype(F32)).astype(BF16)
            ref = dh.at[d, r, c]
            pending[d] = [send(ref, ref, at_z(to_z3))]
        elif s == 6:
            ref = dh.at[d, :, cols(own4, w16)]
            pending[d] = [send(ref, ref, at_z(to_z2))]
        elif s == 7:
            ref = dh.at[d, :, cols(own3, w8)]
            pending[d] = [send(ref, ref, at_z(to_z1))]
        elif s == 8:
            refs = [dh.at[d, :, cols(own2[k], w8)] for k in range(2)]
            pending[d] = [send(refs[k], refs[k], at_y(second_to[k])) for k in range(2)]
        elif s == 9:
            refs = [dh.at[d, :, cols(own1[k], w4)] for k in range(2)]
            pending[d] = [send(refs[k], refs[k], at_y(first_to[k])) for k in range(2)]
        else:
            if d == 0:
                loads[3].wait()
                loads[4].wait()

            def mat(i, total):
                c = cols(i * w4, w4)
                grad = dh[d, :, c].astype(F32)
                total = total + contract((grad * fac_g[d, :, c]).astype(BF16), wg[:, c])
                return total + contract((grad * fac_u[d, :, c]).astype(BF16), wu[:, c])

            total = lax.fori_loop(0, 4, mat, jnp.zeros((ROWS, feat), F32)).astype(BF16)
            if d == 0:
                ret[pl.ds(0, ROWS), :] = total
            else:
                gr[d] = total
                returned[d] = send(
                    gr.at[d], ret.at[pl.ds(d * ROWS, ROWS)], group(lax.rem(zh - d + GROUPS, GROUPS))
                )

    for t in range(max(LAG) + STAGES):
        for k, d in enumerate(ORDER):
            if 0 <= t - LAG[k] < STAGES:
                stage(d, t - LAG[k])

    for d in ORDER[1:]:
        returned[d].wait_recv()
    snd[...] = jnp.dot(perm_back[...], ret[...], preferred_element_type=F32).astype(BF16)
    to_peers = [
        send(snd.at[piece(lax.rem(j + o, PEERS))], rx.at[piece(j)], peer(lax.rem(j + o, PEERS)))
        for o in range(1, PEERS)
    ]
    rx[piece(j), :] = snd[piece(j), :]
    for copy in to_peers:
        copy.wait_recv()
    result[...] = jnp.dot(pick[...], rx[...], preferred_element_type=F32).astype(BF16)
    for copy in started:
        copy.wait_send()


def on_device(d_out, combine, expert_ids, slot_ids, w_gate, w_up, w_down, saved_gate, saved_up):
    feat, hid = w_gate.shape[1:]
    zh = lax.axis_index("node") // PEERS
    distance = (expert_ids // PEERS - zh + GROUPS) % GROUPS
    place = jnp.where(slot_ids >= 0, (expert_ids % PEERS) * PART + distance * CAP + slot_ids, 2 * SLOTS)
    r = np.arange(SLOTS)
    peer, rest = r // PART, r % PART
    target = (rest // CAP) * ROWS + peer * CAP + rest % CAP
    back = np.zeros((SLOTS, SLOTS), np.float32)
    back[r, target] = 1.0
    perm_back = jnp.asarray(back, BF16)
    perm_out = jnp.asarray(back.T, BF16)

    def two(*shape):
        return pltpu.VMEM(shape, BF16)

    def four(*shape):
        return pltpu.VMEM(shape, F32)

    vmem = pl.BlockSpec(memory_space=pltpu.VMEM)
    hbm = pl.BlockSpec(memory_space=pl.ANY)
    g = GROUPS
    return pl.pallas_call(
        kernel,
        out_shape=jax.ShapeDtypeStruct(d_out.shape, BF16),
        in_specs=[vmem] * 6 + [hbm] * 5,
        out_specs=vmem,
        scratch_shapes=[
            two(feat, hid), two(feat, hid), two(hid, feat), two(SLOTS, hid), two(SLOTS, hid),
            four(g, ROWS, hid), four(g, ROWS, hid),
            two(SLOTS, feat), two(SLOTS, feat), two(g, ROWS, feat), two(g, ROWS, feat),
            two(g, ROWS, hid), two(g, 2, ROWS, hid // 4), two(g, 2, ROWS, hid // 8), four(g, 2, ROWS, hid // 8),
            two(g, 2, ROWS, hid // 8), two(g, ROWS, hid // 8), two(g, ROWS, hid // 8), four(g, ROWS, hid // 8),
            two(g, ROWS, hid // 16), two(g, ROWS, hid // 16), four(g, ROWS, hid // 16),
            two(g, ROWS // 2, hid // 16), two(g, ROWS // 2, hid // 16), four(g, ROWS // 2, hid // 16),
            two(g, ROWS, hid), two(g, ROWS, feat), two(SLOTS, feat), two(SLOTS, feat), two(SLOTS, feat),
            two(d_out.shape[0], SLOTS),
            pltpu.SemaphoreType.DMA((5,)), pltpu.SemaphoreType.DMA((NCOPY,)), pltpu.SemaphoreType.DMA((NCOPY,)),
        ],
        compiler_params=pltpu.CompilerParams(
            collective_id=0, has_side_effects=True, vmem_limit_bytes=48 * 1024 * 1024
        ),
        cost_estimate=pl.CostEstimate(flops=1_200_000_000, bytes_accessed=8_000_000, transcendentals=800_000),
    )(
        d_out, place.T, combine.T, place, perm_out, perm_back,
        w_gate[0], w_up[0], w_down[0], saved_gate[0], saved_up[0],
    )


def solution(mesh):
    return jax.shard_map(
        on_device,
        mesh=mesh,
        in_specs=(
            P("node", "local"), P("node", None), P("node", None), P("node", None),
            P("node", "local", None), P("node", "local", None), P("node", None, "local"),
            P("node", None, None), P("node", None, None),
        ),
        out_specs=P("node", "local"),
        check_vma=False,
    )
```

time: 859 us -> 151 us (0.18)
  the two profiles are of different devices: /device:TPU:1 before, /device:TPU:33 now
where the time goes in v1:
time: 151 us; the launch traced here: 150 us
  Pallas kernels  136 us (90%)
  local copies, waits for them, and re-layouts  12 us (8%)
  other arithmetic  2.34 us (2%)
    pallas_call x1, Pallas kernels, on_device(): pl.pallas_call(kernel, out_shape=jax.ShapeDtypeStruct(d_out.shape, BF16),...  136 us
    unnamed x23, local copies, waits for them, and re-layouts  9.83 us

profile of v1, /device:TPU:33, one launch (start us, length us, event | category | flops | bytes accessed | tf_op | source)
XLA Modules:
  0.0 150.1 jit_solution(11221616951263008353)
XLA Ops:
  0.0 0.0 copy-start
  0.0 0.0 copy-start.1
  0.0 0.0 copy-start.9
  0.0 0.8 broadcast_compare_fusion
  0.9 0.7 broadcast_compare_fusion.1
  1.5 0.1 copy.40
  1.7 0.1 copy.35
  1.8 1.5 %copy.43.d_out = bf16[128,224]{1,0:T(8,128)(2,1)} copy(bf16[128,224]{0,1:T(8,128)(2,1)} %param.11) | data formatting | bytes 114688 | tf_op args[0]
  3.4 0.8 copy.32
  4.2 0.1 add_select_fusion.2
  4.3 0.1 copy.36
  4.3 0.1 copy.39
  4.4 0.7 add_add_fusion
  5.1 0.1 copy.41
  5.2 0.1 copy.44.place_row
  5.3 0.0 copy-start.3
  5.3 0.6 copy-done.3
  5.9 1.5 copy.42
  7.4 0.0 copy-done
  7.4 0.0 copy-done.1
  7.4 0.0 copy-done.9
  7.4 0.0 copy-start.2
  7.4 1.2 copy-done.2
  8.6 0.0 copy-start.4
  8.6 0.8 copy-done.4
  9.5 1.0 copy-done.5
  10.4 1.0 copy-done.6
  11.4 0.8 copy-done.7
  12.2 135.7 %shard_map.109 = bf16[128,224]{1,0:T(8,128)(2,1)S(1)} custom-call(bf16[128,224]{1,0:T(8,128)(2,1)S(1)} %copy-done.7, s32[3,128]{1,0:T(4,128)S(1)} %copy.44.place_row, f32[3,128]{1,0:T(4,128)S(1)} %bitcast.12, s32[128,3]{1,0:T(8,128)S(1)} %copy-done.4, bf16[384,384]{1,0:T(8,128)(2,1)S(1)} %copy-done.5, bf16[384,384]{1,0:T(8,128)(2,1)S(1)} %copy-done.6, ...), custom_call_target="tpu_custom_call" | custom-call | flops 1200000000 | bytes 8000000 | tf_op jit(solution)/shard_map/pallas_call | solution.py:275
  147.9 0.0 copy-start.8
  148.0 0.6 copy-done.8
  148.6 1.6 %copy.45 = bf16[128,224]{0,1:T(8,128)(2,1)} copy(bf16[128,224]{1,0:T(8,128)(2,1)} %copy-done.8) | data formatting | bytes 114688 | tf_op jit(solution)/shard_map/pallas_call | solution.py:275
  (4 shorter events, 0.0 us)
Async XLA Ops:
  0.0 7.4 %copy-start = (bf16[1,384,2048]{2,1,0:T(8,128)(2,1)S(1)}, bf16[1,384,2048]{2,1,0:T(8,128)(2,1)}, u32[]{:S(2)}) copy-start(bf16[1,384,2048]{2,1,0:T(8,128)(2,1)} %param.18) | copy-start | bytes 4718596
  0.0 7.4 %copy-start.1 = (bf16[1,224,2048]{2,1,0:T(8,128)(2,1)S(1)}, bf16[1,224,2048]{2,1,0:T(8,128)(2,1)}, u32[]{:S(2)}) copy-start(bf16[1,224,2048]{2,1,0:T(8,128)(2,1)} %param.15) | copy-start | bytes 2752516
  0.0 7.4 %copy-start.9 = (f32[128,3]{0,1:T(4,128)S(1)}, f32[128,3]{0,1:T(4,128)}, u32[]{:S(2)}) copy-start(f32[128,3]{0,1:T(4,128)} %param.12) | copy-start | bytes 4612
  5.3 0.6 copy-start.3
  7.4 1.2 copy-start.2
  8.6 0.8 copy-start.4
  9.5 1.0 copy-start.5
  10.4 1.0 copy-start.6
  11.4 0.8 copy-start.7
  147.9 0.6 copy-start.8

commit v2 on v0

v2 whole, which is shorter than its diff:
```python
import jax
import jax.numpy as jnp
from jax import lax
from jax.experimental import pallas as pl
from jax.experimental.pallas import tpu as pltpu
from jax.sharding import PartitionSpec as P

F32, BF16 = jnp.float32, jnp.bfloat16
GROUPS, PEERS, CAP = 4, 8, 12
ROWS = PEERS * CAP
PART = GROUPS * CAP
SLOTS = GROUPS * ROWS
ORDER = (0, 1, 3, 2)
LAG = (0, 2, 2, 3)
STAGES = 6
NCOPY = 2 * 7 + 2 * 3 + 3 * 3 + GROUPS * 13
MESH = pl.DeviceIdType.MESH


def mul(value, unit):
    return pl.multiple_of(value, unit)


def mat(a, b):
    return jnp.dot(a, b, preferred_element_type=F32)


def contract(a, b, dim):
    return lax.dot_general(a, b, (((dim,), (dim,)), ((), ())), preferred_element_type=F32)


def by_const(value, factor):
    return lax.shift_right_logical(value * factor, jnp.full(value.shape, 16, jnp.int32))


def kernel(
    d_out, combine, experts, slots, wg_hbm, wu_hbm, wd_hbm, sg_hbm, su_hbm,
    result,
    wg, wu, wd, sg, su, fac_g, fac_u, out, x1, zsend, arr, part_f, part, r1, u, xs, xr, dh, yp, yr, yown,
    gr, ret, snd, rx, pick, perm_out, perm_back, load_sem, send_sem, recv_sem,
):
    width = wd.shape[2]
    piece_w = width // 4
    node, local = lax.axis_index("node"), lax.axis_index("local")
    zh, j = lax.div(node, PEERS), lax.rem(node, PEERS)
    zl, y = lax.div(local, 4), lax.rem(local, 4)
    zq, zi = lax.div(zl, 4), lax.rem(zl, 4)

    def cols(start, size):
        return pl.ds(mul(start, 128), size)

    def peer(o):
        return {"node": zh * PEERS + lax.rem(j + o, PEERS), "local": local}

    def group(o):
        return {"node": lax.rem(zh + o, GROUPS) * PEERS + j, "local": local}

    def at_y(o):
        return {"node": node, "local": zl * 4 + lax.rem(y + o, 4)}

    def at_z(o):
        return {"node": node, "local": (zq * 4 + lax.rem(zi + o, 4)) * 4 + y}

    across = {"node": node, "local": ((1 - zq) * 4 + zi) * 4 + y}

    own = cols(y * width, width)
    loads = [
        pltpu.make_async_copy(src, dst, load_sem.at[i])
        for i, (src, dst) in enumerate((
            (wd_hbm.at[:, own], wd.at[y]), (sg_hbm.at[:, own], sg), (su_hbm.at[:, own], su),
            (wg_hbm.at[:, own], wg.at[y]), (wu_hbm.at[:, own], wu.at[y]),
        ))
    ]
    for load in loads:
        load.start()

    barrier = pltpu.get_barrier_semaphore()
    partners = [peer(o) for o in range(1, PEERS)] + [group(o) for o in range(1, GROUPS)]
    partners += [at_y(o) for o in range(1, 4)] + [at_z(o) for o in range(1, 4)] + [across]
    for partner in partners:
        pl.semaphore_signal(barrier, inc=1, device_id=partner, device_id_type=MESH)

    expert, number = experts[...], slots[...]
    eight, three = jnp.full(expert.shape, 3, jnp.int32), jnp.full(expert.shape, 3, jnp.int32)
    distance = lax.bitwise_and(lax.shift_right_logical(expert, eight) - zh + GROUPS, three)
    place = lax.bitwise_and(expert, jnp.full(expert.shape, 7, jnp.int32)) * PART + distance * CAP + number
    place = jnp.where(number >= 0, place, 2 * SLOTS)
    slot = lax.broadcasted_iota(jnp.int32, pick.shape, 0)
    chosen = jnp.zeros(slot.shape, F32)
    weight = jnp.zeros(slot.shape, F32)
    for k in range(3):
        hit = slot == place[k : k + 1, :]
        chosen = chosen + jnp.where(hit, 1.0, 0.0)
        weight = weight + jnp.where(hit, combine[k : k + 1, :], 0.0)
    pick[...] = chosen.astype(BF16)
    weight = jnp.sum(weight, axis=1, keepdims=True)
    out[...] = (contract(pick[...], d_out[...], 1) * weight).astype(BF16)

    row = lax.broadcasted_iota(jnp.int32, perm_out.shape, 0)
    col = lax.broadcasted_iota(jnp.int32, perm_out.shape, 1)
    d_of = by_const(row, 683)
    rest = row - d_of * ROWS
    j_of = by_const(rest, 5462)
    perm_out[...] = jnp.where(col == j_of * PART + d_of * CAP + rest - j_of * CAP, 1.0, 0.0).astype(BF16)

    pl.semaphore_wait(barrier, len(partners))

    started = []

    def send(src, dst, to):
        i = len(started)
        copy = pltpu.make_async_remote_copy(
            src_ref=src, dst_ref=dst, send_sem=send_sem.at[i], recv_sem=recv_sem.at[i], device_id=to, device_id_type=MESH,
        )
        copy.start()
        started.append(copy)
        return copy

    def piece(o):
        return pl.ds(mul(lax.rem(j + o, PEERS) * PART, 16), PART)

    def share(src, dst):
        return [send(src.at[:, cols(lax.rem(y + o, 4) * width, width)], dst.at[y], at_y(o)) for o in range(1, 4)]

    to_peers = [send(out.at[piece(o)], x1.at[piece(0)], peer(o)) for o in range(1, PEERS)]
    x1[piece(0), :] = out[piece(0), :]
    down = share(wd_hbm, wd)
    j_of = by_const(row, 1366)
    rest = row - j_of * PART
    d_of = by_const(rest, 5462)
    perm_back[...] = jnp.where(col == d_of * ROWS + j_of * CAP + rest - d_of * CAP, 1.0, 0.0).astype(BF16)
    for copy in to_peers:
        copy.wait_recv()
    sorted_rows = mat(perm_out[...], x1[...]).astype(BF16)
    to_groups = {}
    for d in ORDER[1:]:
        zsend[d] = sorted_rows[d * ROWS : (d + 1) * ROWS]
        to_groups[d] = send(zsend.at[d], arr.at[d, y], group(d))
    arr[0, y] = sorted_rows[:ROWS]

    pending = {}
    returned = []

    def stage(d, s):
        if s == 0:
            if d:
                to_groups[d].wait_recv()
            pending[d] = [send(arr.at[d, y], arr.at[d, y], at_y(o)) for o in range(1, 4)]
            if d == 0:
                pending["weights"] = share(wg_hbm, wg) + share(wu_hbm, wu)
                loads[1].wait()
                loads[2].wait()

                def factors(i, carry):
                    e = lax.div(i, ROWS // 16)
                    source = lax.rem(zh - e + GROUPS, GROUPS) * ROWS
                    inner = lax.rem(i, ROWS // 16) * 16
                    gate = sg[pl.ds(mul(source + inner, 16), 16), :].astype(F32)
                    up = su[pl.ds(mul(source + inner, 16), 16), :].astype(F32)
                    sig = 1.0 / (1.0 + jnp.exp(-gate))
                    to = pl.ds(mul(i * 16, 16), 16)
                    fac_g[to, :] = up * sig * (1.0 + gate * (1.0 - sig))
                    fac_u[to, :] = gate * sig
                    return carry

                lax.fori_loop(0, SLOTS // 16, factors, 0)
            return
        for copy in pending[d]:
            copy.wait_recv()
        if s == 1:
            if d == 0:
                loads[0].wait()
                for copy in down:
                    copy.wait_recv()
            total = mat(arr[d, 0], wd[0])
            for k in range(1, 4):
                total = total + mat(arr[d, k], wd[k])
            part_f[d] = total
            part[d] = total.astype(BF16)
            pending[d] = [
                send(part.at[d, :, cols(lax.rem(zi + o, 4) * piece_w, piece_w)], r1.at[d, o], at_z(o)) for o in range(1, 4)
            ]
        elif s == 2:
            total = part_f[d, :, cols(zi * piece_w, piece_w)]
            for o in range(1, 4):
                total = total + r1[d, o].astype(F32)
            xs[d] = total.astype(BF16)
            pending[d] = [send(xs.at[d], xr.at[d], across)]
            u[d] = total
        elif s == 3:
            c = cols(zi * piece_w, piece_w)
            dh[d, :, c] = (u[d] + xr[d].astype(F32)).astype(BF16)
            ref = dh.at[d, :, c]
            pending[d] = [send(ref, ref, at_z(o)) for o in range(1, 4)]
        elif s == 4:
            grad = dh[d].astype(F32)
            r = pl.ds(d * ROWS, ROWS)
            grad_gate = (grad * fac_g[r, :]).astype(BF16)
            grad_up = (grad * fac_u[r, :]).astype(BF16)
            if d == 0:
                loads[3].wait()
                loads[4].wait()
                for copy in pending["weights"]:
                    copy.wait_recv()
            pending[d] = []
            for o in (1, 2, 3, 0):
                k = lax.rem(y + o, 4)
                total = contract(grad_gate, wg[k], 1) + contract(grad_up, wu[k], 1)
                if o:
                    yp[d, o] = total.astype(BF16)
                    pending[d].append(send(yp.at[d, o], yr.at[d, o], at_y(o)))
                else:
                    yown[d] = total
        else:
            total = yown[d]
            for o in range(1, 4):
                total = total + yr[d, o].astype(F32)
            r = pl.ds(d * ROWS, ROWS)
            if d == 0:
                ret[r, :] = total.astype(BF16)
            else:
                gr[d] = total.astype(BF16)
                returned.append(send(gr.at[d], ret.at[r], group(GROUPS - d)))

    for t in range(max(LAG) + STAGES):
        for k, d in enumerate(ORDER):
            if 0 <= t - LAG[k] < STAGES:
                stage(d, t - LAG[k])

    for copy in returned:
        copy.wait_recv()
    snd[...] = mat(perm_back[...], ret[...]).astype(BF16)
    to_peers = [send(snd.at[piece(o)], rx.at[piece(0)], peer(o)) for o in range(1, PEERS)]
    rx[piece(0), :] = snd[piece(0), :]
    for copy in to_peers:
        copy.wait_recv()
    result[...] = contract(rx[...], pick[...], 0).astype(BF16)
    for copy in started:
        copy.wait_send()


def on_device(d_out, combine, expert_ids, slot_ids, w_gate, w_up, w_down, saved_gate, saved_up):
    feat, hid = w_gate.shape[1:]
    tokens = d_out.shape[0]
    w = hid // 4

    def two(*shape):
        return pltpu.VMEM(shape, BF16)

    def four(*shape):
        return pltpu.VMEM(shape, F32)

    vmem = pl.BlockSpec(memory_space=pltpu.VMEM)
    hbm = pl.BlockSpec(memory_space=pl.ANY)
    g = GROUPS
    return pl.pallas_call(
        kernel,
        out_shape=jax.ShapeDtypeStruct((feat, tokens), BF16),
        in_specs=[vmem] * 4 + [hbm] * 5,
        out_specs=vmem,
        scratch_shapes=[
            two(4, feat, w), two(4, feat, w), two(4, feat, w), two(SLOTS, w), two(SLOTS, w), four(SLOTS, w), four(SLOTS, w),
            two(SLOTS, feat), two(SLOTS, feat), two(g, ROWS, feat), two(g, 4, ROWS, feat),
            four(g, ROWS, w), two(g, ROWS, w), two(g, 4, ROWS, w // 4), four(g, ROWS, w // 4),
            two(g, ROWS, w // 4), two(g, ROWS, w // 4), two(g, ROWS, w),
            two(g, 4, ROWS, feat), two(g, 4, ROWS, feat), four(g, ROWS, feat),
            two(g, ROWS, feat), two(SLOTS, feat), two(SLOTS, feat), two(SLOTS, feat),
            two(SLOTS, tokens), two(SLOTS, SLOTS), two(SLOTS, SLOTS),
            pltpu.SemaphoreType.DMA((5,)), pltpu.SemaphoreType.DMA((NCOPY,)), pltpu.SemaphoreType.DMA((NCOPY,)),
        ],
        compiler_params=pltpu.CompilerParams(
            collective_id=0, has_side_effects=True, vmem_limit_bytes=60 * 1024 * 1024
        ),
        cost_estimate=pl.CostEstimate(flops=1_200_000_000, bytes_accessed=8_000_000, transcendentals=800_000),
    )(
        d_out.T, combine.T, expert_ids.T, slot_ids.T,
        w_gate[0], w_up[0], w_down[0].T, saved_gate[0], saved_up[0],
    ).T


def solution(mesh):
    return jax.shard_map(
        on_device,
        mesh=mesh,
        in_specs=(
            P("node", "local"), P("node", None), P("node", None), P("node", None),
            P("node", "local", None), P("node", "local", None), P("node", None, "local"),
            P("node", None, None), P("node", None, None),
        ),
        out_specs=P("node", "local"),
        check_vma=False,
    )
```

time: 859 us -> 116 us (0.14)
  the two profiles are of different devices: /device:TPU:1 before, /device:TPU:65 now
where the time goes in v2:
time: 116 us
  Pallas kernels  115 us (99%)
  local copies, waits for them, and re-layouts  1.45 us (1%)
    pallas_call x1, Pallas kernels, on_device(): pl.pallas_call(kernel, out_shape=jax.ShapeDtypeStruct((feat, tokens), BF1...  115 us

profile of v2, /device:TPU:65, one launch (start us, length us, event | category | flops | bytes accessed | tf_op | source)
XLA Modules:
  0.0 116.2 jit_solution(3722524434552311556)
XLA Ops:
  0.0 114.8 %shard_map.91 = bf16[224,128]{1,0:T(8,128)(2,1)} custom-call(bf16[224,128]{1,0:T(8,128)(2,1)} %bitcast.18, f32[3,128]{1,0:T(4,128)} %bitcast.19, s32[3,128]{1,0:T(4,128)} %bitcast.20, s32[3,128]{1,0:T(4,128)} %bitcast.21, bf16[224,2048]{1,0:T(8,128)(2,1)} %bitcast.14, bf16[224,2048]{1,0:T(8,128)(2,1)} %bitcast.15, bf16[224,2048]{1,0:T(8,128)(2,1)} %bitcast.16, ...), custom_call_target="tpu_custom_call" | custom-call | flops 1200000000 | bytes 8000000 | tf_op jit(solution)/shard_map/pallas_call | solution.py:256
  114.8 1.4 %copy.11 = bf16[128,224]{0,1:T(8,128)(2,1)} copy(bf16[128,224]{0,1:T(8,128)(2,1)} %bitcast.17) | data formatting | bytes 114688

commit v3 on v2

--- a/solution.py
+++ b/solution.py
@@ -11,8 +11,10 @@
 PART = GROUPS * CAP
 SLOTS = GROUPS * ROWS
 ORDER = (0, 1, 3, 2)
-LAG = (0, 2, 2, 3)
+LAG = (0, 3, 3, 3)
 STAGES = 6
+FIRST = 1
+HOLD = 6
 NCOPY = 2 * 7 + 2 * 3 + 3 * 3 + GROUPS * 13
 MESH = pl.DeviceIdType.MESH
 
@@ -37,7 +39,7 @@
     d_out, combine, experts, slots, wg_hbm, wu_hbm, wd_hbm, sg_hbm, su_hbm,
     result,
     wg, wu, wd, sg, su, fac_g, fac_u, out, x1, zsend, arr, part_f, part, r1, u, xs, xr, dh, yp, yr, yown,
-    gr, ret, snd, rx, pick, perm_out, perm_back, load_sem, send_sem, recv_sem,
+    gr, ret, snd, rx, pick, perm_out, perm_back, load_sem, send_sem, recv_sem, far_sem,
 ):
     width = wd.shape[2]
     piece_w = width // 4
@@ -75,7 +77,7 @@
         load.start()
 
     barrier = pltpu.get_barrier_semaphore()
-    partners = [peer(o) for o in range(1, PEERS)] + [group(o) for o in range(1, GROUPS)]
+    partners = [peer(o) for o in range(1, PEERS)] + [group(1), group(3)]
     partners += [at_y(o) for o in range(1, 4)] + [at_z(o) for o in range(1, 4)] + [across]
     for partner in partners:
         pl.semaphore_signal(barrier, inc=1, device_id=partner, device_id_type=MESH)
@@ -104,6 +106,8 @@
     perm_out[...] = jnp.where(col == j_of * PART + d_of * CAP + rest - j_of * CAP, 1.0, 0.0).astype(BF16)
 
     pl.semaphore_wait(barrier, len(partners))
+    for o in (1, 3):
+        pl.semaphore_signal(far_sem.at[o], inc=1, device_id=group(o), device_id_type=MESH)
 
     started = []
 
@@ -135,6 +139,9 @@
     to_groups = {}
     for d in ORDER[1:]:
         zsend[d] = sorted_rows[d * ROWS : (d + 1) * ROWS]
+        if d == 2:
+            for o in (1, 3):
+                pl.semaphore_wait(far_sem.at[o], 1)
         to_groups[d] = send(zsend.at[d], arr.at[d, y], group(d))
     arr[0, y] = sorted_rows[:ROWS]
 
@@ -197,7 +204,7 @@
             r = pl.ds(d * ROWS, ROWS)
             grad_gate = (grad * fac_g[r, :]).astype(BF16)
             grad_up = (grad * fac_u[r, :]).astype(BF16)
-            if d == 0:
+            if d == FIRST:
                 loads[3].wait()
                 loads[4].wait()
                 for copy in pending["weights"]:
@@ -222,10 +229,9 @@
                 gr[d] = total.astype(BF16)
                 returned.append(send(gr.at[d], ret.at[r], group(GROUPS - d)))
 
-    for t in range(max(LAG) + STAGES):
-        for k, d in enumerate(ORDER):
-            if 0 <= t - LAG[k] < STAGES:
-                stage(d, t - LAG[k])
+    work = [(s + LAG[k] + (HOLD if d == 0 and s >= 4 else 0), k, d, s) for k, d in enumerate(ORDER) for s in range(STAGES)]
+    for _, _, d, s in sorted(work):
+        stage(d, s)
 
     for copy in returned:
         copy.wait_recv()
@@ -267,6 +273,7 @@
             two(g, ROWS, feat), two(SLOTS, feat), two(SLOTS, feat), two(SLOTS, feat),
             two(SLOTS, tokens), two(SLOTS, SLOTS), two(SLOTS, SLOTS),
             pltpu.SemaphoreType.DMA((5,)), pltpu.SemaphoreType.DMA((NCOPY,)), pltpu.SemaphoreType.DMA((NCOPY,)),
+            pltpu.SemaphoreType.REGULAR((4,)),
         ],
         compiler_params=pltpu.CompilerParams(
             collective_id=0, has_side_effects=True, vmem_limit_bytes=60 * 1024 * 1024

time: 116 us -> 112 us (0.966)
  the two profiles are of different devices: /device:TPU:65 before, /device:TPU:1 now
where the time goes in v3:
time: 112 us
  Pallas kernels  110 us (98%)
  local copies, waits for them, and re-layouts  1.45 us (1%)
    pallas_call x1, Pallas kernels, on_device(): pl.pallas_call(kernel, out_shape=jax.ShapeDtypeStruct((feat, tokens), BF1...  110 us

profile of v3, /device:TPU:1, one launch (start us, length us, event | category | flops | bytes accessed | tf_op | source)
XLA Modules:
  0.0 111.7 jit_solution(5625216369386417452)
XLA Ops:
  0.0 110.2 %shard_map.91 = bf16[224,128]{1,0:T(8,128)(2,1)} custom-call(bf16[224,128]{1,0:T(8,128)(2,1)} %bitcast.18, f32[3,128]{1,0:T(4,128)} %bitcast.19, s32[3,128]{1,0:T(4,128)} %bitcast.20, s32[3,128]{1,0:T(4,128)} %bitcast.21, bf16[224,2048]{1,0:T(8,128)(2,1)} %bitcast.14, bf16[224,2048]{1,0:T(8,128)(2,1)} %bitcast.15, bf16[224,2048]{1,0:T(8,128)(2,1)} %bitcast.16, ...), custom_call_target="tpu_custom_call" | custom-call | flops 1200000000 | bytes 8000000 | tf_op jit(solution)/shard_map/pallas_call | solution.py:262
  110.2 1.4 %copy.11 = bf16[128,224]{0,1:T(8,128)(2,1)} copy(bf16[128,224]{0,1:T(8,128)(2,1)} %bitcast.17) | data formatting | bytes 114688

commit v4 on v3

--- a/solution.py
+++ b/solution.py
@@ -10,12 +10,12 @@
 ROWS = PEERS * CAP
 PART = GROUPS * CAP
 SLOTS = GROUPS * ROWS
-ORDER = (0, 1, 3, 2)
+CHUNKS = ((0, 0, 96), (2, 0, 96), (1, 0, 96), (3, 0, 96))
 LAG = (0, 3, 3, 3)
 STAGES = 6
+HOLD = 6
 FIRST = 1
-HOLD = 6
-NCOPY = 2 * 7 + 2 * 3 + 3 * 3 + GROUPS * 13
+NCOPY = 2 * 7 + 3 * 3 + len(CHUNKS) * 15
 MESH = pl.DeviceIdType.MESH
 
 
@@ -39,7 +39,7 @@
     d_out, combine, experts, slots, wg_hbm, wu_hbm, wd_hbm, sg_hbm, su_hbm,
     result,
     wg, wu, wd, sg, su, fac_g, fac_u, out, x1, zsend, arr, part_f, part, r1, u, xs, xr, dh, yp, yr, yown,
-    gr, ret, snd, rx, pick, perm_out, perm_back, load_sem, send_sem, recv_sem, far_sem,
+    gr, ret, snd, rx, pick, perm_out, perm_back, wd_all, wg_all, wu_all, load_sem, send_sem, recv_sem, far_sem,
 ):
     width = wd.shape[2]
     piece_w = width // 4
@@ -71,6 +71,7 @@
         for i, (src, dst) in enumerate((
             (wd_hbm.at[:, own], wd.at[y]), (sg_hbm.at[:, own], sg), (su_hbm.at[:, own], su),
             (wg_hbm.at[:, own], wg.at[y]), (wu_hbm.at[:, own], wu.at[y]),
+            (wd_hbm, wd_all), (wg_hbm, wg_all), (wu_hbm, wu_all),
         ))
     ]
     for load in loads:
@@ -128,7 +129,8 @@
 
     to_peers = [send(out.at[piece(o)], x1.at[piece(0)], peer(o)) for o in range(1, PEERS)]
     x1[piece(0), :] = out[piece(0), :]
-    down = share(wd_hbm, wd)
+    loads[5].wait()
+    down = share(wd_all, wd)
     j_of = by_const(row, 1366)
     rest = row - j_of * PART
     d_of = by_const(rest, 5462)
@@ -137,24 +139,32 @@
         copy.wait_recv()
     sorted_rows = mat(perm_out[...], x1[...]).astype(BF16)
     to_groups = {}
-    for d in ORDER[1:]:
-        zsend[d] = sorted_rows[d * ROWS : (d + 1) * ROWS]
-        if d == 2:
+    zsend[...] = sorted_rows
+    arr[y, 0:ROWS, :] = sorted_rows[:ROWS]
+    far = True
+    for n, (d, low, count) in enumerate(CHUNKS):
+        if d == 2 and far:
+            far = False
             for o in (1, 3):
                 pl.semaphore_wait(far_sem.at[o], 1)
-        to_groups[d] = send(zsend.at[d], arr.at[d, y], group(d))
-    arr[0, y] = sorted_rows[:ROWS]
+        if d:
+            r = pl.ds(d * ROWS + low, count)
+            to_groups[n] = send(zsend.at[r], arr.at[y, r], group(d))
 
     pending = {}
     returned = []
 
-    def stage(d, s):
+    def stage(n, s):
+        d, low, count = CHUNKS[n]
+        r = pl.ds(d * ROWS + low, count)
         if s == 0:
             if d:
-                to_groups[d].wait_recv()
-            pending[d] = [send(arr.at[d, y], arr.at[d, y], at_y(o)) for o in range(1, 4)]
-            if d == 0:
-                pending["weights"] = share(wg_hbm, wg) + share(wu_hbm, wu)
+                to_groups[n].wait_recv()
+            pending[n] = [send(arr.at[y, r], arr.at[y, r], at_y(o)) for o in range(1, 4)]
+            if n == 0:
+                loads[6].wait()
+                loads[7].wait()
+                pending["weights"] = share(wg_all, wg) + share(wu_all, wu)
                 loads[1].wait()
                 loads[2].wait()
 
@@ -172,66 +182,64 @@
 
                 lax.fori_loop(0, SLOTS // 16, factors, 0)
             return
-        for copy in pending[d]:
+        for copy in pending[n]:
             copy.wait_recv()
         if s == 1:
-            if d == 0:
+            if n == 0:
                 loads[0].wait()
                 for copy in down:
                     copy.wait_recv()
-            total = mat(arr[d, 0], wd[0])
+            total = mat(arr[0, r, :], wd[0])
             for k in range(1, 4):
-                total = total + mat(arr[d, k], wd[k])
-            part_f[d] = total
-            part[d] = total.astype(BF16)
-            pending[d] = [
-                send(part.at[d, :, cols(lax.rem(zi + o, 4) * piece_w, piece_w)], r1.at[d, o], at_z(o)) for o in range(1, 4)
+                total = total + mat(arr[k, r, :], wd[k])
+            part_f[r, :] = total
+            part[r, :] = total.astype(BF16)
+            pending[n] = [
+                send(part.at[r, cols(lax.rem(zi + o, 4) * piece_w, piece_w)], r1.at[o, r], at_z(o)) for o in range(1, 4)
             ]
         elif s == 2:
-            total = part_f[d, :, cols(zi * piece_w, piece_w)]
+            total = part_f[r, cols(zi * piece_w, piece_w)]
             for o in range(1, 4):
-                total = total + r1[d, o].astype(F32)
-            xs[d] = total.astype(BF16)
-            pending[d] = [send(xs.at[d], xr.at[d], across)]
-            u[d] = total
+                total = total + r1[o, r, :].astype(F32)
+            xs[r, :] = total.astype(BF16)
+            pending[n] = [send(xs.at[r], xr.at[r], across)]
+            u[r, :] = total
         elif s == 3:
             c = cols(zi * piece_w, piece_w)
-            dh[d, :, c] = (u[d] + xr[d].astype(F32)).astype(BF16)
-            ref = dh.at[d, :, c]
-            pending[d] = [send(ref, ref, at_z(o)) for o in range(1, 4)]
+            dh[r, c] = (u[r, :] + xr[r, :].astype(F32)).astype(BF16)
+            ref = dh.at[r, c]
+            pending[n] = [send(ref, ref, at_z(o)) for o in range(1, 4)]
         elif s == 4:
-            grad = dh[d].astype(F32)
-            r = pl.ds(d * ROWS, ROWS)
+            grad = dh[r, :].astype(F32)
             grad_gate = (grad * fac_g[r, :]).astype(BF16)
             grad_up = (grad * fac_u[r, :]).astype(BF16)
-            if d == FIRST:
+            if n == FIRST:
                 loads[3].wait()
                 loads[4].wait()
                 for copy in pending["weights"]:
                     copy.wait_recv()
-            pending[d] = []
+            pending[n] = []
             for o in (1, 2, 3, 0):
                 k = lax.rem(y + o, 4)
                 total = contract(grad_gate, wg[k], 1) + contract(grad_up, wu[k], 1)
                 if o:
-                    yp[d, o] = total.astype(BF16)
-                    pending[d].append(send(yp.at[d, o], yr.at[d, o], at_y(o)))
+                    yp[o, r, :] = total.astype(BF16)
+                    pending[n].append(send(yp.at[o, r], yr.at[o, r], at_y(o)))
                 else:
-                    yown[d] = total
+                    yown[r, :] = total
         else:
-            total = yown[d]
+            total = yown[r, :]
             for o in range(1, 4):
-                total = total + yr[d, o].astype(F32)
-            r = pl.ds(d * ROWS, ROWS)
-            if d == 0:
+                total = total + yr[o, r, :].astype(F32)
+            if n == 0:
                 ret[r, :] = total.astype(BF16)
             else:
-                gr[d] = total.astype(BF16)
-                returned.append(send(gr.at[d], ret.at[r], group(GROUPS - d)))
-
-    work = [(s + LAG[k] + (HOLD if d == 0 and s >= 4 else 0), k, d, s) for k, d in enumerate(ORDER) for s in range(STAGES)]
-    for _, _, d, s in sorted(work):
-        stage(d, s)
+                gr[r, :] = total.astype(BF16)
+                returned.append(send(gr.at[r], ret.at[r], group(GROUPS - d)))
+
+    work = [(s + LAG[n] + (HOLD if n == 0 and s >= 4 else 0), n, s) for n in range(len(CHUNKS)) for s in range(STAGES)]
+    for _, n, s in sorted(work):
+        stage(n, s)
 
     for copy in returned:
         copy.wait_recv()
@@ -258,7 +266,6 @@
 
     vmem = pl.BlockSpec(memory_space=pltpu.VMEM)
     hbm = pl.BlockSpec(memory_space=pl.ANY)
-    g = GROUPS
     return pl.pallas_call(
         kernel,
         out_shape=jax.ShapeDtypeStruct((feat, tokens), BF16),
@@ -266,13 +273,14 @@
         out_specs=vmem,
         scratch_shapes=[
             two(4, feat, w), two(4, feat, w), two(4, feat, w), two(SLOTS, w), two(SLOTS, w), four(SLOTS, w), four(SLOTS, w),
-            two(SLOTS, feat), two(SLOTS, feat), two(g, ROWS, feat), two(g, 4, ROWS, feat),
-            four(g, ROWS, w), two(g, ROWS, w), two(g, 4, ROWS, w // 4), four(g, ROWS, w // 4),
-            two(g, ROWS, w // 4), two(g, ROWS, w // 4), two(g, ROWS, w),
-            two(g, 4, ROWS, feat), two(g, 4, ROWS, feat), four(g, ROWS, feat),
-            two(g, ROWS, feat), two(SLOTS, feat), two(SLOTS, feat), two(SLOTS, feat),
+            two(SLOTS, feat), two(SLOTS, feat), two(SLOTS, feat), two(4, SLOTS, feat),
+            four(SLOTS, w), two(SLOTS, w), two(4, SLOTS, w // 4), four(SLOTS, w // 4),
+            two(SLOTS, w // 4), two(SLOTS, w // 4), two(SLOTS, w),
+            two(4, SLOTS, feat), two(4, SLOTS, feat), four(SLOTS, feat),
+            two(SLOTS, feat), two(SLOTS, feat), two(SLOTS, feat), two(SLOTS, feat),
             two(SLOTS, tokens), two(SLOTS, SLOTS), two(SLOTS, SLOTS),
-            pltpu.SemaphoreType.DMA((5,)), pltpu.SemaphoreType.DMA((NCOPY,)), pltpu.SemaphoreType.DMA((NCOPY,)),
+            two(feat, hid), two(feat, hid), two(feat, hid),
+            pltpu.SemaphoreType.DMA((8,)), pltpu.SemaphoreType.DMA((NCOPY,)), pltpu.SemaphoreType.DMA((NCOPY,)),
             pltpu.SemaphoreType.REGULAR((4,)),
         ],
         compiler_params=pltpu.CompilerParams(

time: 112 us -> 111 us (level)
    pallas_call x1, Pallas kernels: 110 us -> 109 us  [on_device(): pl.pallas_call(kernel, out_shape=jax.ShapeDtypeStruct((feat, tokens), BF1...]
where the time goes in v4:
time: 111 us; the launch traced here: 110 us
  Pallas kernels  109 us (98%)
  local copies, waits for them, and re-layouts  1.45 us (1%)
    pallas_call x1, Pallas kernels, on_device(): pl.pallas_call(kernel, out_shape=jax.ShapeDtypeStruct((feat, tokens), BF1...  109 us

profile of v4, /device:TPU:1, one launch (start us, length us, event | category | flops | bytes accessed | tf_op | source)
XLA Modules:
  0.0 110.1 jit_solution(83315502155367361)
XLA Ops:
  0.0 108.7 %shard_map.91 = bf16[224,128]{1,0:T(8,128)(2,1)} custom-call(bf16[224,128]{1,0:T(8,128)(2,1)} %bitcast.18, f32[3,128]{1,0:T(4,128)} %bitcast.19, s32[3,128]{1,0:T(4,128)} %bitcast.20, s32[3,128]{1,0:T(4,128)} %bitcast.21, bf16[224,2048]{1,0:T(8,128)(2,1)} %bitcast.14, bf16[224,2048]{1,0:T(8,128)(2,1)} %bitcast.15, bf16[224,2048]{1,0:T(8,128)(2,1)} %bitcast.16, ...), custom_call_target="tpu_custom_call" | custom-call | flops 1200000000 | bytes 8000000 | tf_op jit(solution)/shard_map/pallas_call | solution.py:269
  108.7 1.4 %copy.11 = bf16[128,224]{0,1:T(8,128)(2,1)} copy(bf16[128,224]{0,1:T(8,128)(2,1)} %bitcast.17) | data formatting | bytes 114688
